TPU v7x, 32 devices: a whole 2x2x4 slice. The times are simulated.
32 devices in a mesh: seq: 4 (over y, x), ctx: 8 (over z, core).
Axes of the slice: x: 2, y: 2, z: 4, core: 2. Of those that a mesh axis runs over, the one named last changes fastest.
Arguments:
- inputs: bfloat16 [4, 1024, 1024], P('seq', 'ctx'), may hold values from -6 to 6
- w_query: bfloat16 [1024, 1024], replicated, may hold values from -0.1875 to 0.1875
- w_key: bfloat16 [1024, 1024], replicated, as said below
- w_value: bfloat16 [1024, 1024], replicated, may hold values from -0.1875 to 0.1875
- damping: float32 [8, 128], replicated, may hold values from 0.25 to 4
- grad_out: bfloat16 [4, 1024, 1024], P('seq', 'ctx'), may hold values from -6 to 6
Outputs:
- grad_inputs: bfloat16 [4, 1024, 1024], P('seq', 'ctx')
- grad_weights: float32 [1024, 1024], P(('seq', 'ctx'))
Inputs may be any that keep to these rules, and one draw needn't show every extreme that they name: `w_key`: entries scaled by a random factor per column.
All inputs are finite; a program needn't handle non-finite values.
Results may differ from a plain program's by a relative error of at most 0.013.
Values sent between devices are 32-bit elements; how exact they have to be, the bound alone decides.
A program may use at most 256 MiB of HBM per device.

v0:
```python
import jax
import jax.numpy as jnp
from jax import lax
from jax.sharding import PartitionSpec as P

ITERS = 2


EPSILON = 1e-06
EXACT_PRECISION = lax.Precision.HIGHEST


def entering(value, axis, join, neutral, backward):
    count, mine = (lax.axis_size(axis), lax.axis_index(axis))
    pieces = jax.tree.map(lambda part: lax.all_gather(part, axis), value)
    if backward:
        pieces = jax.tree.map(lambda part: part[::-1], pieces)
        mine = count - 1 - mine
    running = jax.tree.map(
        lambda part, zero: jnp.full_like(part, 0) + jnp.asarray(zero, part.dtype), value, neutral
    )

    def step(position, running):
        longer = join(running, jax.tree.map(lambda part: part[position], pieces))
        return jax.tree.map(lambda new, old: jnp.where(position < mine, new, old), longer, running)

    return lax.fori_loop(0, count - 1, step, running)


def unit_rows(tensor):
    inv_norm = lax.rsqrt(jnp.sum(tensor * tensor, axis=-1, keepdims=True) + EPSILON)
    return (tensor * inv_norm, inv_norm)


def unit_back(normed, inv_norm, upstream_gradient):
    return (
        upstream_gradient - normed * jnp.sum(normed * upstream_gradient, axis=-1, keepdims=True)
    ) * inv_norm


def causal_mask(length):
    rows_idx = lax.broadcasted_iota(jnp.int32, (length, length), 0)
    cols_idx = lax.broadcasted_iota(jnp.int32, (length, length), 1)
    return (rows_idx >= cols_idx).astype(jnp.float32)


def apply_system(vector, key_inputs, prior_state, damping, causal):
    inner = jnp.einsum("htk,hsk->hts", vector, key_inputs, precision=EXACT_PRECISION) * causal
    result = jnp.einsum("hkj,htj->htk", prior_state, vector, precision=EXACT_PRECISION)
    result = result + jnp.einsum("hts,hsk->htk", inner, key_inputs, precision=EXACT_PRECISION)
    return result + damping[:, None, :] * vector


def conjugate(target, key_inputs, prior_state, damping, causal):
    solution = jnp.zeros_like(target)
    residual = target
    direction = target
    norm_now = jnp.sum(residual * residual, axis=-1, keepdims=True)
    for sweep in range(ITERS):
        image_vec = apply_system(direction, key_inputs, prior_state, damping, causal)
        step_size = norm_now / (jnp.sum(direction * image_vec, axis=-1, keepdims=True) + EPSILON)
        solution = solution + step_size * direction
        residual = residual - step_size * image_vec
        norm_next = jnp.sum(residual * residual, axis=-1, keepdims=True)
        direction = residual + norm_next / (norm_now + EPSILON) * direction
        norm_now = norm_next
    return solution


def add_pair(earlier, later):
    return (earlier[0] + later[0], earlier[1] + later[1])


def mesa_heads(query_rows, key_rows, value_inputs, upstream_gradient, damping):
    length = query_rows.shape[1]
    causal = causal_mask(length)
    normed_q, inv_q = unit_rows(query_rows)
    key_inputs, inv_k = unit_rows(key_rows)
    gram_local = jnp.einsum("htk,htj->hkj", key_inputs, key_inputs, precision=EXACT_PRECISION)
    cross_term_local = jnp.einsum(
        "htv,htk->hvk", value_inputs, key_inputs, precision=EXACT_PRECISION
    )
    gram_prior, cross_prior = entering(
        (gram_local, cross_term_local),
        "ctx",
        add_pair,
        (jnp.zeros_like(gram_local), jnp.zeros_like(cross_term_local)),
        False,
    )
    query_solution = conjugate(normed_q, key_inputs, gram_prior, damping, causal)
    scores = (
        jnp.einsum("htv,hsv->hts", upstream_gradient, value_inputs, precision=EXACT_PRECISION)
        * causal
    )
    adjoint_rhs = jnp.einsum(
        "hvk,htv->htk", cross_prior, upstream_gradient, precision=EXACT_PRECISION
    )
    adjoint_rhs = adjoint_rhs + jnp.einsum(
        "hts,hsk->htk", scores, key_inputs, precision=EXACT_PRECISION
    )
    adjoint = conjugate(adjoint_rhs, key_inputs, gram_prior, damping, causal)
    answer_cross_term = jnp.einsum(
        "sip,sig->spg", query_solution, upstream_gradient, precision=EXACT_PRECISION
    )
    gram_half = jnp.einsum("htk,htj->hkj", adjoint, query_solution, precision=EXACT_PRECISION)
    answer_gram = gram_half + jnp.swapaxes(gram_half, 1, 2)
    cross_term_after, gram_after = entering(
        (answer_cross_term, answer_gram),
        "ctx",
        add_pair,
        (jnp.zeros_like(answer_cross_term), jnp.zeros_like(answer_gram)),
        True,
    )
    query_keys = (
        jnp.einsum("htk,hsk->hts", query_solution, key_inputs, precision=EXACT_PRECISION) * causal
    )
    adjoint_keys = (
        jnp.einsum("htk,hsk->hts", adjoint, key_inputs, precision=EXACT_PRECISION) * causal
    )
    key_gradient = jnp.einsum(
        "zrp,zwp->zwr", cross_term_after, value_inputs, precision=EXACT_PRECISION
    )
    key_gradient = key_gradient + jnp.einsum(
        "hts,htk->hsk", scores, query_solution, precision=EXACT_PRECISION
    )
    key_gradient = key_gradient - jnp.einsum(
        "hkj,hsj->hsk", gram_after, key_inputs, precision=EXACT_PRECISION
    )
    key_gradient = key_gradient - jnp.einsum(
        "hts,htk->hsk", query_keys, adjoint, precision=EXACT_PRECISION
    )
    key_gradient = key_gradient - jnp.einsum(
        "hts,htk->hsk", adjoint_keys, query_solution, precision=EXACT_PRECISION
    )
    value_gradient = jnp.einsum(
        "zgf,ztg->ztf", cross_term_after, key_inputs, precision=EXACT_PRECISION
    )
    value_gradient = value_gradient + jnp.einsum(
        "hts,htv->hsv", query_keys, upstream_gradient, precision=EXACT_PRECISION
    )
    return (
        unit_back(normed_q, inv_q, adjoint),
        unit_back(key_inputs, inv_k, key_gradient),
        value_gradient,
    )


def heads_of(tensor, head_count):
    length = tensor.shape[0]
    return tensor.astype(jnp.float32).reshape(length, head_count, -1).transpose(1, 0, 2)


def rows_of(tensor):
    head_count, length, size_k = tensor.shape
    return tensor.transpose(1, 0, 2).reshape(length, head_count * size_k)


def on_device(inputs, w_query, w_key, w_value, damping, grad_out):
    local_rows = inputs[0]
    head_count = damping.shape[0]
    query_all = jnp.dot(local_rows, w_query, preferred_element_type=jnp.float32).astype(
        jnp.bfloat16
    )
    key_all = jnp.dot(local_rows, w_key, preferred_element_type=jnp.float32).astype(jnp.bfloat16)
    value_all = jnp.dot(local_rows, w_value, preferred_element_type=jnp.float32).astype(
        jnp.bfloat16
    )
    query_heads = heads_of(query_all, head_count)
    key_heads = heads_of(key_all, head_count)
    value_heads = heads_of(value_all, head_count)
    upstream_heads = heads_of(grad_out[0], head_count)
    query_grad, key_gradient, value_gradient = mesa_heads(
        query_heads, key_heads, value_heads, upstream_heads, damping
    )
    query_cols = rows_of(query_grad).astype(jnp.bfloat16)
    key_cols = rows_of(key_gradient).astype(jnp.bfloat16)
    value_cols = rows_of(value_gradient).astype(jnp.bfloat16)
    contract = (((1,), (1,)), ((), ()))
    summed = lax.dot_general(query_cols, w_query, contract, preferred_element_type=jnp.float32)
    summed = summed + lax.dot_general(key_cols, w_key, contract, preferred_element_type=jnp.float32)
    summed = summed + lax.dot_general(
        value_cols, w_value, contract, preferred_element_type=jnp.float32
    )
    grad_inputs = summed.astype(jnp.bfloat16)[None]
    seq_rows = lax.psum_scatter(
        lax.dot_general(
            local_rows, key_cols, (((0,), (0,)), ((), ())), preferred_element_type=jnp.float32
        ),
        "seq",
        scatter_dimension=0,
        tiled=True,
    )
    grad_weights = lax.psum_scatter(seq_rows, "ctx", scatter_dimension=0, tiled=True)
    return (grad_inputs, grad_weights)


def solution(mesh):
    in_specs = (P("seq", "ctx", None), P(), P(), P(), P(), P("seq", "ctx", None))
    out_specs = (P("seq", "ctx", None), P(("seq", "ctx"), None))
    return jax.shard_map(
        on_device, mesh=mesh, in_specs=in_specs, out_specs=out_specs, check_vma=False
    )
```

profile of v0, /device:TPU:0, one launch (start us, length us, event | category | flops | bytes accessed | tf_op | source)
XLA Modules:
  0.0 368.0 jit_solution(15814575135249083259)
XLA Ops:
  23.8 40.6 %all-gather.9.cloned.1.call-done = f32[64,128,128]{2,1,0:T(8,128)} async-done(((f32[8,128,128]{2,1,0:T(8,128)}), f32[64,128,128]{2,1,0:T(8,128)}) %all-gather.9.cloned.1.call-update) | async-done | bytes 4194320 | tf_op jit(solution)/shard_map/all_gather | solution.py:15
  64.3 47.5 %all-gather.11.cloned.1.call-done = f32[64,128,128]{2,1,0:T(8,128)} async-done(((f32[8,128,128]{2,1,0:T(8,128)}), f32[64,128,128]{2,1,0:T(8,128)}) %all-gather.11.cloned.1.call-update) | async-done | bytes 4194320 | tf_op jit(solution)/shard_map/all_gather | solution.py:15
  111.8 18.4 %while.32 = (s32[]{:T(128)}, f32[8,128,128]{2,1,0:T(8,128)}, f32[8,128,128]{2,1,0:T(8,128)}, s32[]{:T(128)}, f32[8,8,128,128]{3,2,1,0:T(8,128)}, /*index=5*/f32[8,8,128,128]{3,2,1,0:T(8,128)}, s32[]{:T(128)}, s32[]{:T(128)}) while((s32[]{:T(128)}, f32[8,128,128]{2,1,0:T(8,128)}, f32[8,128,128]{2,1,0:T(8,128)}, s32[]{:T(128)}, ...), condition=%wide.region_2.3_spmd.clone, body=%wide.region_1.0_spmd.clone.sunk | while | flops 786436 | bytes 3145845 | solution.py:27
  114.2 2.7 add_select_fusion.6
  116.9 2.7 add_select_fusion.6
  119.5 2.7 add_select_fusion.6
  122.2 2.7 add_select_fusion.6
  124.9 2.7 add_select_fusion.6
  127.6 2.7 add_select_fusion.6
  131.9 2.7 bitcast_add_fusion.3
  147.4 3.2 fusion.48
  154.9 2.8 convolution_multiply_fusion.1
  157.8 2.9 convolution_multiply_fusion
  160.6 32.6 %all-gather.13.cloned.1.call-done = f32[64,128,128]{2,1,0:T(8,128)} async-done(((f32[8,128,128]{2,1,0:T(8,128)}), f32[64,128,128]{2,1,0:T(8,128)}) %all-gather.13.cloned.1.call-update) | async-done | bytes 4194320 | tf_op jit(solution)/shard_map/all_gather | solution.py:15
  193.2 4.6 %rev.6 = f32[8,8,128,128]{3,2,1,0:T(8,128)} reverse(f32[8,8,128,128]{3,2,1,0:T(8,128)} %bitcast.193), dimensions={0} | reverse | bytes 8388608 | tf_op jit(solution)/shard_map/rev | solution.py:17
  197.8 42.7 %all-gather.15.cloned.1.call-done = f32[64,128,128]{2,1,0:T(8,128)} async-done(((f32[8,128,128]{2,1,0:T(8,128)}), f32[64,128,128]{2,1,0:T(8,128)}) %all-gather.15.cloned.1.call-update) | async-done | bytes 4194320 | tf_op jit(solution)/shard_map/all_gather | solution.py:15
  240.5 4.7 %rev.7 = f32[8,8,128,128]{3,2,1,0:T(8,128)} reverse(f32[8,8,128,128]{3,2,1,0:T(8,128)} %bitcast.194), dimensions={0} | reverse | bytes 8388608 | tf_op jit(solution)/shard_map/rev | solution.py:17
  245.2 18.2 %while.33 = (s32[]{:T(128)}, f32[8,128,128]{2,1,0:T(8,128)}, f32[8,128,128]{2,1,0:T(8,128)}, s32[]{:T(128)}, f32[8,8,128,128]{3,2,1,0:T(8,128)}, /*index=5*/f32[8,8,128,128]{3,2,1,0:T(8,128)}, s32[]{:T(128)}, s32[]{:T(128)}) while((s32[]{:T(128)}, f32[8,128,128]{2,1,0:T(8,128)}, f32[8,128,128]{2,1,0:T(8,128)}, s32[]{:T(128)}, ...), condition=%wide.region_14.15_spmd.clone, body=%wide.region_13.14_spmd.clone.sunk | while | flops 786436 | bytes 3145845 | solution.py:27
  247.5 2.6 add_select_fusion.7
  250.2 2.6 add_select_fusion.7
  252.8 2.6 add_select_fusion.7
  255.5 2.6 add_select_fusion.7
  274.7 51.2 %reduce-scatter.5.cloned.1.call-done = f32[256,1024]{0,1:T(8,128)} async-done(((f32[1024,1024]{0,1:T(8,128)}), f32[256,1024]{0,1:T(8,128)}) %reduce-scatter.5.cloned.1.call-update) | async-done | bytes 1048592 | tf_op jit(solution)/shard_map/reduce_scatter | solution.py:185
  337.1 24.0 %reduce-scatter.7.cloned.1.call-done = f32[32,1024]{1,0:T(8,128)} async-done(((f32[256,1024]{1,0:T(8,128)}), f32[32,1024]{1,0:T(8,128)}) %reduce-scatter.7.cloned.1.call-update) | async-done | bytes 131088
  (115 shorter events, 67.2 us)
Async XLA Ops:
  7.2 2.6 copy-start
  7.2 2.6 copy-start.13
  7.2 57.2 %all-gather.9.cloned.1.call-start = ((), (), s32[]{:S(2)}) async-start(), calls=%async_computation.3 | async-start | bytes 4718592 | tf_op jit(solution)/shard_map/all_gather | solution.py:15
  14.3 97.5 %all-gather.11.cloned.1.call-start = ((), (), s32[]{:S(2)}) async-start(), calls=%async_computation.4 | async-start | bytes 4718592 | tf_op jit(solution)/shard_map/all_gather | solution.py:15
  18.7 174.4 %all-gather.13.cloned.1.call-start = ((), (), s32[]{:S(2)}) async-start(), calls=%async_computation.5 | async-start | bytes 4718592 | tf_op jit(solution)/shard_map/all_gather | solution.py:15
  131.9 3.7 %copy-start.10 = (f32[8,128,128]{2,1,0:T(8,128)}, f32[8,128,128]{2,1,0:T(8,128)S(1)}, u32[]{:S(2)}) copy-start(f32[8,128,128]{2,1,0:T(8,128)S(1)} %fusion.42) | copy-start | bytes 1572868
  131.9 3.7 %copy-start.1 = (f32[8,128,128]{2,1,0:T(8,128)S(1)}, f32[8,128,128]{2,1,0:T(8,128)}, u32[]{:S(2)}) copy-start(f32[8,128,128]{2,1,0:T(8,128)} %get-tuple-element.223) | copy-start | bytes 1572868
  134.6 2.3 copy-start.19
  137.6 1.1 copy-start.8
  138.7 1.7 copy-start.18
  144.9 0.8 copy-start.4
  147.2 93.4 %all-gather.15.cloned.1.call-start = ((), (), s32[]{:S(2)}) async-start(), calls=%async_computation.6 | async-start | bytes 4718592 | tf_op jit(solution)/shard_map/all_gather | solution.py:15
  154.8 171.1 %reduce-scatter.5.cloned.1.call-start = ((), (), s32[]{:S(2)}) async-start(), calls=%async_computation.2 | async-start | bytes 5242880 | tf_op jit(solution)/shard_map/reduce_scatter | solution.py:185
  263.4 4.4 %copy-start.3 = (f32[8,128,128]{2,1,0:T(8,128)S(1)}, f32[8,128,128]{2,1,0:T(8,128)}, u32[]{:S(2)}) copy-start(f32[8,128,128]{2,1,0:T(8,128)} %get-tuple-element.225) | copy-start | bytes 1572868
  265.3 3.2 copy-start.7
  265.3 3.2 copy-start.11
  267.8 1.9 copy-start.5
  267.8 1.9 copy-start.17
  269.7 2.1 copy-start.14
  274.4 86.7 %reduce-scatter.7.cloned.1.call-start = ((), (), s32[]{:S(2)}) async-start(), calls=%async_computation.7 | async-start | bytes 1179648
  330.2 2.6 copy-start.2
  332.0 1.9 copy-start.9
  332.0 1.9 copy-start.16
  333.9 1.6 copy-start.6
  (2 other events, 1.4 us)
Sparse Core Ops, SparseCore 0:
  14.5 49.8 all-gather.8
  65.9 45.8 all-gather.10
  147.3 45.8 all-gather.12
  194.6 45.8 all-gather.14
  274.5 51.3 reduce-scatter.4
  328.8 32.3 reduce-scatter.6
where the time goes:
time: 369 us; the launch traced here: 368 us
  waiting for transfers between devices  239 us (65%)
  matrix products  51.9 us (14%)
  other arithmetic  42.5 us (12%)
  local copies, waits for them, and re-layouts  19.5 us (5%)
  between operations  14.7 us (4%)
    all_gather x4, waiting for transfers between devices, entering(): pieces = jax.tree.map(lambda part: lax.all_gather(part, axis), value)  163 us
    reduce_scatter x1, waiting for transfers between devices, on_device(): lax.psum_scatter(lax.dot_general(local_rows, key_cols, (((0,), (0,)), (()...  51.2 us
    select_n x14, other arithmetic, step(): jnp.where(position < mine, new, old)  36.6 us
    unnamed x7, waiting for transfers between devices  24.1 us
    rev x2, local copies, waits for them, and re-layouts, entering(): pieces = jax.tree.map(lambda part: part[::-1], pieces)  9.29 us
  transfers between devices with their start and end apart: 6, of which 6 were waited for; matrix products, arithmetic and copies ran while one was open for 9% of the time, Pallas kernels for 0%

commit v1 on v0

v1 whole, which is shorter than its diff:
```python
import functools

import jax
import jax.numpy as jnp
from jax import lax
from jax.experimental import pallas as pl
from jax.experimental.pallas import tpu as pltpu
from jax.sharding import PartitionSpec as P

EPSILON = 1e-06
MESH = pl.DeviceIdType.MESH
F32 = jnp.float32
BF16 = jnp.bfloat16
NN = (((1,), (0,)), ((), ()))
NT = (((1,), (1,)), ((), ()))
TN = (((0,), (0,)), ((), ()))


def split(tensor, exact):
    high = tensor.astype(BF16)
    if not exact or tensor.dtype == BF16:
        return (high,)
    return (high, (tensor - high.astype(F32)).astype(BF16))


def mm(a, b, dims, exact=False):
    a_terms, b_terms = split(a, exact), split(b, exact)
    total = lax.dot_general(a_terms[0], b_terms[0], dims, preferred_element_type=F32)
    for term in a_terms[1:]:
        total += lax.dot_general(term, b_terms[0], dims, preferred_element_type=F32)
    for term in b_terms[1:]:
        total += lax.dot_general(a_terms[0], term, dims, preferred_element_type=F32)
    return total


def row_dot(a, b):
    return jnp.sum(a * b, axis=-1, keepdims=True)


def solve(target, keys, gram, damping, causal):
    def apply(vector):
        inner = mm(vector, keys, NT) * causal
        return mm(vector, gram, NN) + mm(inner, keys, NN) + damping * vector

    norm = row_dot(target, target)
    image = apply(target)
    step = norm / (row_dot(target, image) + EPSILON)
    answer = step * target
    residual = target - step * image
    norm_next = row_dot(residual, residual)
    direction = residual + norm_next / (norm + EPSILON) * target
    image = apply(direction)
    step = norm_next / (row_dot(direction, image) + EPSILON)
    return answer + step * direction


def unit_back(normed, inv_norm, upstream):
    return (upstream - normed * row_dot(normed, upstream)) * inv_norm


def kernel(
    ns, nz,
    x_ref, wq_ref, wk_ref, wv_ref, damp_ref, g_ref,
    gi_ref, gw_ref,
    wbuf, xf, xb, xt, gsend, gf,
    qn, rq, kn, rk, val, grad,
    loc_a, in_a, out_a, loc_b, in_b, out_b,
    dk_part, dv_part, dqkv,
    part, seq_recv, reduced, z_recv, fin, fin_recv, gi_acc, gi_recv,
    wsem, swap_send, swap_recv, a_send, a_recv, b_send, b_recv,
    s_send, s_recv, z_send, z_recv_sem, e_send, e_recv,
):
    s = lax.axis_index("seq")
    c = lax.axis_index("ctx")
    core = lax.rem(c, 2)
    chip = c // 2
    sib = c + 1 - 2 * core
    tok, width = x_ref.shape
    heads, _, size = kn.shape
    half = heads * size
    own_cols = pl.ds(pl.multiple_of(core * half, half), half)
    sib_cols = pl.ds(pl.multiple_of((1 - core) * half, half), half)
    own_rows = pl.ds(pl.multiple_of(core * tok, tok), tok)
    sib_rows = pl.ds(pl.multiple_of((1 - core) * tok, tok), tok)
    seq_block = width // ns
    z_block = seq_block // nz
    fin_rows = z_block // 2

    def remote(src, dst, send, recv, seq_id, ctx_id):
        return pltpu.make_async_remote_copy(
            src_ref=src, dst_ref=dst, send_sem=send, recv_sem=recv,
            device_id=(seq_id, ctx_id), device_id_type=MESH,
        )

    weights = [
        pltpu.make_async_copy(ref.at[:, own_cols], wbuf.at[i], wsem.at[i])
        for i, ref in enumerate((wk_ref, wv_ref, wq_ref))
    ]
    for copy in weights:
        copy.start()

    barrier = pltpu.get_barrier_semaphore()
    pl.semaphore_signal(barrier, inc=1, device_id=(s, sib), device_id_type=MESH)

    def greet_seq(i, carry):
        pl.semaphore_signal(
            barrier, inc=1, device_id=(lax.rem(s + i, ns), c), device_id_type=MESH
        )
        return carry

    def greet_z(i, carry):
        pl.semaphore_signal(
            barrier, inc=1, device_id=(s, lax.rem(chip + i, nz) * 2 + core), device_id_type=MESH
        )
        return carry

    lax.fori_loop(1, ns, greet_seq, 0)
    lax.fori_loop(1, nz, greet_z, 0)

    xf[own_rows, :] = x_ref[...].astype(F32)
    gsend[...] = g_ref[:, sib_cols].astype(F32)
    gf[own_rows, :] = g_ref[:, own_cols].astype(F32)
    pl.semaphore_wait(barrier, 1 + (ns - 1) + (nz - 1))

    swap_x = remote(xf.at[own_rows], xf.at[own_rows], swap_send.at[0], swap_recv.at[0], s, sib)
    swap_g = remote(gsend, gf.at[own_rows], swap_send.at[1], swap_recv.at[1], s, sib)
    swap_x.start()
    swap_g.start()

    @pl.when(chip == 0)
    def _():
        in_a[...] = jnp.zeros_like(in_a)

    @pl.when(chip == nz - 1)
    def _():
        in_b[...] = jnp.zeros_like(in_b)

    swap_x.wait()
    xb[...] = xf[...].astype(BF16)
    weights[0].wait()
    keys_all = jnp.dot(xb[...], wbuf[0], preferred_element_type=F32).astype(BF16).astype(F32)
    weights[1].wait()
    vals_all = jnp.dot(xb[...], wbuf[1], preferred_element_type=F32).astype(BF16)

    def unit(tensor):
        inv = lax.rsqrt(row_dot(tensor, tensor) + EPSILON)
        return tensor * inv, inv

    def link_a(h):
        return remote(out_a.at[h], in_a.at[h], a_send.at[h], a_recv.at[h], s, c + 2)

    def link_b(h):
        return remote(out_b.at[h], in_b.at[h], b_send.at[h], b_recv.at[h], s, c - 2)

    for h in range(heads):
        cols = slice(h * size, (h + 1) * size)
        normed, inv = unit(keys_all[:, cols])
        kn[h] = normed
        rk[h] = inv
        val[h] = vals_all[:, cols]
        local = mm(jnp.concatenate([normed, vals_all[:, cols].astype(F32)], axis=1), normed, TN)
        loc_a[h] = local

        @pl.when(chip == 0)
        def _():
            out_a[h] = local
            if nz > 1:
                link_a(h).start()

    weights[2].wait()
    query_all = jnp.dot(xb[...], wbuf[2], preferred_element_type=F32).astype(BF16).astype(F32)
    swap_g.wait()
    for h in range(heads):
        cols = slice(h * size, (h + 1) * size)
        normed, inv = unit(query_all[:, cols])
        qn[h] = normed
        rq[h] = inv
        grad[h] = gf[:, cols].astype(BF16)
    xt[...] = xf[...].T.astype(BF16)

    tokens = 2 * tok
    row_ids = lax.broadcasted_iota(jnp.int32, (tokens, tokens), 0)
    col_ids = lax.broadcasted_iota(jnp.int32, (tokens, tokens), 1)

    def first_pass(h, carry):
        @pl.when(chip > 0)
        def _():
            link_a(h).wait_recv()

            @pl.when(chip < nz - 1)
            def _():
                out_a[h] = in_a[h] + loc_a[h]
                link_a(h).start()

        causal = (row_ids >= col_ids).astype(F32)
        causal_t = (row_ids <= col_ids).astype(F32)
        causal_two = jnp.concatenate([causal, causal], axis=0)
        causal_two_t = jnp.concatenate([causal_t, causal_t], axis=1)
        keys, values, upstream = kn[h], val[h], grad[h]
        gram = in_a[h, :size, :]
        cross = in_a[h, size:, :]
        damping = damp_ref[pl.ds(core * heads + h, 1), :]
        scores = mm(upstream, values, NT) * causal
        rhs = mm(upstream, cross, NN) + mm(scores, keys, NN)
        answer = solve(jnp.concatenate([qn[h], rhs], axis=0), keys, gram, damping, causal_two)
        z, u = answer[:tokens], answer[tokens:]
        half_gram = mm(jnp.concatenate([u, z], axis=0), answer, TN)
        local = jnp.concatenate([half_gram, mm(z, upstream, TN)], axis=0)
        loc_b[h] = local

        @pl.when(chip == nz - 1)
        def _():
            out_b[h] = local
            if nz > 1:
                link_b(h).start()

        answer_keys = mm(keys, answer, NT) * causal_two_t
        zk_t, uk_t = answer_keys[:, :tokens], answer_keys[:, tokens:]
        scores_t = mm(values, upstream, NT) * causal_t
        dk_part[h] = mm(jnp.concatenate([scores_t - uk_t, -zk_t], axis=1), answer, NN)
        dv_part[h] = mm(zk_t, upstream, NN)
        dqkv[0, h] = unit_back(qn[h], rq[h], u).astype(BF16)
        return carry

    lax.fori_loop(0, heads, first_pass, 0)

    def seq_copy(h, i):
        peer = lax.rem(s + i, ns)
        rows = pl.ds(pl.multiple_of(peer * seq_block, seq_block), seq_block)
        return remote(
            part.at[h, rows], seq_recv.at[h, i - 1], s_send.at[h, i - 1], s_recv.at[h, i - 1],
            peer, c,
        )

    def z_copy(h, i):
        peer = lax.rem(chip + i, nz)
        rows = pl.ds(pl.multiple_of(peer * z_block, z_block), z_block)
        return remote(
            reduced.at[h, rows], z_recv.at[h, i - 1], z_send.at[h, i - 1],
            z_recv_sem.at[h, i - 1], s, peer * 2 + core,
        )

    def second_pass(h, carry):
        @pl.when(chip < nz - 1)
        def _():
            link_b(h).wait_recv()

            @pl.when(chip > 0)
            def _():
                out_b[h] = in_b[h] + loc_b[h]
                link_b(h).start()

        keys = kn[h]
        gram = in_b[h, :size, :]
        cross = in_b[h, size:, :]
        dk = dk_part[h] + mm(val[h], cross, NT) - mm(keys, gram, NN)
        dv = dv_part[h] + mm(keys, cross, NN)
        dk = unit_back(keys, rk[h], dk).astype(BF16)
        dqkv[1, h] = dk
        dqkv[2, h] = dv.astype(BF16)
        part[h] = jnp.dot(xt[...], dk, preferred_element_type=F32)
        for i in range(1, ns):
            seq_copy(h, i).start()
        return carry

    lax.fori_loop(0, heads, second_pass, 0)

    def flat(i):
        return jnp.concatenate([dqkv[i, h] for h in range(heads)], axis=1)

    total = lax.dot_general(flat(0), wbuf[2], NT, preferred_element_type=F32)
    total += lax.dot_general(flat(1), wbuf[0], NT, preferred_element_type=F32)
    total += lax.dot_general(flat(2), wbuf[1], NT, preferred_element_type=F32)
    gi_acc[...] = total
    swap_gi = remote(gi_acc.at[sib_rows], gi_recv, e_send.at[0], e_recv.at[0], s, sib)
    swap_gi.start()

    own_seq = pl.ds(pl.multiple_of(s * seq_block, seq_block), seq_block)

    def seq_reduce(h, carry):
        total = part[h, own_seq, :]
        for i in range(1, ns):
            seq_copy(h, i).wait_recv()
            total += seq_recv[h, i - 1]
        reduced[h] = total

        def send(i, carry):
            z_copy(h, i).start()
            return carry

        lax.fori_loop(1, nz, send, 0)
        return carry

    lax.fori_loop(0, heads, seq_reduce, 0)

    swap_gi.wait()
    gi_ref[...] = (gi_acc[own_rows, :] + gi_recv[...]).astype(BF16)

    own_z = pl.ds(pl.multiple_of(chip * z_block, z_block), z_block)
    for h in range(heads):

        def add(i, total):
            z_copy(h, i).wait_recv()
            return total + z_recv[h, i - 1]

        total = lax.fori_loop(1, nz, add, reduced[h, own_z, :])
        fin[:, h * size:(h + 1) * size] = total
    swap_fin = remote(fin, fin_recv, e_send.at[1], e_recv.at[1], s, sib)
    swap_fin.start()
    gw_ref[:, own_cols] = jnp.where(core == 0, fin[:fin_rows, :], fin[fin_rows:, :])

    def drain(h, carry):
        @pl.when(chip < nz - 1)
        def _():
            link_a(h).wait_send()

        @pl.when(chip > 0)
        def _():
            link_b(h).wait_send()

        for i in range(1, ns):
            seq_copy(h, i).wait_send()

        def z_wait(i, carry):
            z_copy(h, i).wait_send()
            return carry

        lax.fori_loop(1, nz, z_wait, 0)
        return carry

    lax.fori_loop(0, heads, drain, 0)
    swap_fin.wait()
    gw_ref[:, sib_cols] = jnp.where(core == 0, fin_recv[:fin_rows, :], fin_recv[fin_rows:, :])


def on_device(ns, nz, inputs, w_query, w_key, w_value, damping, grad_out):
    x, g = inputs[0], grad_out[0]
    tok, width = x.shape
    heads, size = damping.shape[0] // 2, damping.shape[1]
    tokens, half = 2 * tok, heads * size
    seq_block = width // ns
    z_block = seq_block // nz
    vmem = pltpu.VMEM
    dma = pltpu.SemaphoreType.DMA
    state = vmem((heads, 2 * size, size), F32)
    rows32 = vmem((heads, tokens, size), F32)
    rows16 = vmem((heads, tokens, size), BF16)
    norms = vmem((heads, tokens, 1), F32)
    spec = pl.BlockSpec(memory_space=pltpu.VMEM)
    hbm = pl.BlockSpec(memory_space=pl.ANY)
    grad_inputs, grad_weights = pl.pallas_call(
        functools.partial(kernel, ns, nz),
        out_shape=(
            jax.ShapeDtypeStruct((tok, width), BF16),
            jax.ShapeDtypeStruct((z_block // 2, width), F32),
        ),
        in_specs=[spec, hbm, hbm, hbm, spec, spec],
        out_specs=(spec, spec),
        scratch_shapes=[
            vmem((3, width, half), BF16),
            vmem((tokens, width), F32),
            vmem((tokens, width), BF16),
            vmem((width, tokens), BF16),
            vmem((tok, half), F32),
            vmem((tokens, half), F32),
            rows32, norms, rows32, norms, rows16, rows16,
            state, state, state, state, state, state,
            rows32, rows32,
            vmem((3, heads, tokens, size), BF16),
            vmem((heads, width, size), F32),
            vmem((heads, ns - 1, seq_block, size), F32),
            vmem((heads, seq_block, size), F32),
            vmem((heads, nz - 1, z_block, size), F32),
            vmem((z_block, half), F32),
            vmem((z_block, half), F32),
            vmem((tokens, width), F32),
            vmem((tok, width), F32),
            dma((3,)), dma((2,)), dma((2,)),
            dma((heads,)), dma((heads,)), dma((heads,)), dma((heads,)),
            dma((heads, ns - 1)), dma((heads, ns - 1)),
            dma((heads, nz - 1)), dma((heads, nz - 1)),
            dma((2,)), dma((2,)),
        ],
        compiler_params=pltpu.CompilerParams(
            collective_id=0, has_side_effects=True, vmem_limit_bytes=56 * 1024 * 1024
        ),
        name="mesa_backward",
    )(x, w_query, w_key, w_value, damping, g)
    return grad_inputs[None], grad_weights


def solution(mesh):
    in_specs = (P("seq", "ctx", None), P(), P(), P(), P(), P("seq", "ctx", None))
    out_specs = (P("seq", "ctx", None), P(("seq", "ctx"), None))
    return jax.shard_map(
        functools.partial(on_device, mesh.shape["seq"], mesh.shape["ctx"] // 2),
        mesh=mesh, in_specs=in_specs, out_specs=out_specs, check_vma=False,
    )
```

time: 369 us -> 68.8 us (0.19)
  waiting for transfers between devices: 239 us -> 0 us
  Pallas kernels: 0 us -> 63.8 us
  matrix products: 51.9 us -> 0 us
  other arithmetic: 42.5 us -> 0 us
  local copies, waits for them, and re-layouts: 19.5 us -> 3.24 us
  between operations: 14.7 us -> 0.64 us
    all_gather x4 -> x0, waiting for transfers between devices: 163 us -> none  [entering(): pieces = jax.tree.map(lambda part: lax.all_gather(part, axis), value)]
    pallas_call x0 -> x1, Pallas kernels: none -> 63.8 us  [on_device(): pl.pallas_call(functools.partial(kernel, ns, nz), out_shape=(jax.ShapeDty...]
    dot_general x35 -> x0, matrix products: 51.9 us -> none  [the longest x4 4.86 us: apply_system(): jnp.einsum('htk,hsk->hts', vector, key_inputs, precision=EXACT_PRECISION)]
    reduce_scatter x1 -> x0, waiting for transfers between devices: 51.2 us -> none  [on_device(): lax.psum_scatter(lax.dot_general(local_rows, key_cols, (((0,), (0,)), (()...]
    select_n x14 -> x0, other arithmetic: 36.6 us -> none  [step(): jnp.where(position < mine, new, old)]
    unnamed x7 -> x0, waiting for transfers between devices: 24.1 us -> none
    rev x2 -> x0, local copies, waits for them, and re-layouts: 9.29 us -> none  [entering(): pieces = jax.tree.map(lambda part: part[::-1], pieces)]
  transfers between devices with their start and end apart: 6 -> 0, of which waited for: 6 -> 0; matrix products, arithmetic and copies ran while one was open for 9% -> 0% of each run, Pallas kernels for 0% -> 0%
where the time goes in v1:
time: 68.8 us; the launch traced here: 67.6 us
  Pallas kernels  63.8 us (93%)
  local copies, waits for them, and re-layouts  3.24 us (5%)
    pallas_call x1, Pallas kernels, on_device(): pl.pallas_call(functools.partial(kernel, ns, nz), out_shape=(jax.ShapeDty...  63.8 us
    unnamed x2, local copies, waits for them, and re-layouts  3.24 us

profile of v1, /device:TPU:0, one launch (start us, length us, event | category | flops | bytes accessed | tf_op | source)
XLA Modules:
  0.0 67.6 jit_solution(7799946678647702238)
XLA Ops:
  0.6 63.8 %mesa_backward.1 = (bf16[128,1024]{1,0:T(8,128)(2,1)}, f32[32,1024]{1,0:T(8,128)}) custom-call(bf16[128,1024]{1,0:T(8,128)(2,1)} %bitcast.3, bf16[1024,1024]{1,0:T(8,128)(2,1)} %wq_ref.1, bf16[1024,1024]{1,0:T(8,128)(2,1)} %wk_ref.1, bf16[1024,1024]{1,0:T(8,128)(2,1)} %wv_ref.1, f32[8,128]{1,0:T(8,128)} %damp_ref.1, bf16[128,1024]{1,0:T(8,128)(2,1)} %bitcast.4), custom_call_target="tpu_custom_call" | custom-call | tf_op jit(solution)/shard_map/mesa_backward/pallas_call | solution.py:351
  64.4 1.7 %copy.10 = bf16[1,128,1024]{2,1,0:T(8,128)(2,1)} copy(bf16[1,128,1024]{2,1,0:T(8,128)(2,1)} %bitcast.5) | data formatting | bytes 524288
  66.1 1.6 %copy.11 = f32[32,1024]{1,0:T(8,128)} copy(f32[32,1024]{1,0:T(8,128)} %get-tuple-element.9) | data formatting | bytes 262144

commit v2 on v1

--- a/solution.py
+++ b/solution.py
@@ -66,7 +66,7 @@
     qn, rq, kn, rk, val, grad,
     loc_a, in_a, out_a, loc_b, in_b, out_b,
     dk_part, dv_part, dqkv,
-    part, seq_recv, reduced, z_recv, fin, fin_recv, gi_acc, gi_recv,
+    part, halved, passed, quartered, reduced, z_recv, fin, fin_recv, gi_acc, gi_recv,
     wsem, swap_send, swap_recv, a_send, a_recv, b_send, b_recv,
     s_send, s_recv, z_send, z_recv_sem, e_send, e_recv,
 ):
@@ -102,11 +102,8 @@
     barrier = pltpu.get_barrier_semaphore()
     pl.semaphore_signal(barrier, inc=1, device_id=(s, sib), device_id_type=MESH)
 
-    def greet_seq(i, carry):
-        pl.semaphore_signal(
-            barrier, inc=1, device_id=(lax.rem(s + i, ns), c), device_id_type=MESH
-        )
-        return carry
+    for peer in (lax.rem(s + 2, ns), s + 1 - 2 * lax.rem(s, 2)):
+        pl.semaphore_signal(barrier, inc=1, device_id=(peer, c), device_id_type=MESH)
 
     def greet_z(i, carry):
         pl.semaphore_signal(
@@ -114,13 +111,12 @@
         )
         return carry
 
-    lax.fori_loop(1, ns, greet_seq, 0)
     lax.fori_loop(1, nz, greet_z, 0)
 
     xf[own_rows, :] = x_ref[...].astype(F32)
     gsend[...] = g_ref[:, sib_cols].astype(F32)
     gf[own_rows, :] = g_ref[:, own_cols].astype(F32)
-    pl.semaphore_wait(barrier, 1 + (ns - 1) + (nz - 1))
+    pl.semaphore_wait(barrier, 1 + 2 + (nz - 1))
 
     swap_x = remote(xf.at[own_rows], xf.at[own_rows], swap_send.at[0], swap_recv.at[0], s, sib)
     swap_g = remote(gsend, gf.at[own_rows], swap_send.at[1], swap_recv.at[1], s, sib)
@@ -146,11 +142,19 @@
         inv = lax.rsqrt(row_dot(tensor, tensor) + EPSILON)
         return tensor * inv, inv
 
-    def link_a(h):
-        return remote(out_a.at[h], in_a.at[h], a_send.at[h], a_recv.at[h], s, c + 2)
-
-    def link_b(h):
-        return remote(out_b.at[h], in_b.at[h], b_send.at[h], b_recv.at[h], s, c - 2)
+    states = (slice(0, size), slice(size, 2 * size))
+
+    def link_a(h, k):
+        rows = pl.ds(k * size, size)
+        return remote(
+            out_a.at[h, rows], in_a.at[h, rows], a_send.at[h, k], a_recv.at[h, k], s, c + 2
+        )
+
+    def link_b(h, k):
+        rows = pl.ds(k * size, size)
+        return remote(
+            out_b.at[h, rows], in_b.at[h, rows], b_send.at[h, k], b_recv.at[h, k], s, c - 2
+        )
 
     for h in range(heads):
         cols = slice(h * size, (h + 1) * size)
@@ -165,7 +169,8 @@
         def _():
             out_a[h] = local
             if nz > 1:
-                link_a(h).start()
+                link_a(h, 0).start()
+                link_a(h, 1).start()
 
     weights[2].wait()
     query_all = jnp.dot(xb[...], wbuf[2], preferred_element_type=F32).astype(BF16).astype(F32)
@@ -185,12 +190,13 @@
     def first_pass(h, carry):
         @pl.when(chip > 0)
         def _():
-            link_a(h).wait_recv()
-
-            @pl.when(chip < nz - 1)
-            def _():
-                out_a[h] = in_a[h] + loc_a[h]
-                link_a(h).start()
+            for k, rows in enumerate(states):
+                link_a(h, k).wait_recv()
+
+                @pl.when(chip < nz - 1)
+                def _():
+                    out_a[h, rows, :] = in_a[h, rows, :] + loc_a[h, rows, :]
+                    link_a(h, k).start()
 
         causal = (row_ids >= col_ids).astype(F32)
         causal_t = (row_ids <= col_ids).astype(F32)
@@ -212,7 +218,8 @@
         def _():
             out_b[h] = local
             if nz > 1:
-                link_b(h).start()
+                link_b(h, 0).start()
+                link_b(h, 1).start()
 
         answer_keys = mm(keys, answer, NT) * causal_two_t
         zk_t, uk_t = answer_keys[:, :tokens], answer_keys[:, tokens:]
@@ -224,13 +231,19 @@
 
     lax.fori_loop(0, heads, first_pass, 0)
 
-    def seq_copy(h, i):
-        peer = lax.rem(s + i, ns)
-        rows = pl.ds(pl.multiple_of(peer * seq_block, seq_block), seq_block)
-        return remote(
-            part.at[h, rows], seq_recv.at[h, i - 1], s_send.at[h, i - 1], s_recv.at[h, i - 1],
-            peer, c,
-        )
+    high, low = s // 2, lax.rem(s, 2)
+    other_high, other_low = 1 - high, 1 - low
+
+    def halve(parity, h):
+        if parity == 0:
+            src, peer = part.at[h, other_high], other_high * 2 + low
+        else:
+            src, peer = part.at[h, :, other_low], high * 2 + other_low
+        return remote(src, halved.at[h], s_send.at[h, 0], s_recv.at[h, 0], peer, c)
+
+    def quarter(parity, h):
+        peer = high * 2 + other_low if parity == 0 else other_high * 2 + low
+        return remote(passed.at[h], quartered.at[h], s_send.at[h, 1], s_recv.at[h, 1], peer, c)
 
     def z_copy(h, i):
         peer = lax.rem(chip + i, nz)
@@ -240,15 +253,16 @@
             z_recv_sem.at[h, i - 1], s, peer * 2 + core,
         )
 
-    def second_pass(h, carry):
+    def second_pass(parity, h):
         @pl.when(chip < nz - 1)
         def _():
-            link_b(h).wait_recv()
-
-            @pl.when(chip > 0)
-            def _():
-                out_b[h] = in_b[h] + loc_b[h]
-                link_b(h).start()
+            for k, rows in enumerate(states):
+                link_b(h, k).wait_recv()
+
+                @pl.when(chip > 0)
+                def _():
+                    out_b[h, rows, :] = in_b[h, rows, :] + loc_b[h, rows, :]
+                    link_b(h, k).start()
 
         keys = kn[h]
         gram = in_b[h, :size, :]
@@ -258,12 +272,42 @@
         dk = unit_back(keys, rk[h], dk).astype(BF16)
         dqkv[1, h] = dk
         dqkv[2, h] = dv.astype(BF16)
-        part[h] = jnp.dot(xt[...], dk, preferred_element_type=F32)
-        for i in range(1, ns):
-            seq_copy(h, i).start()
-        return carry
-
-    lax.fori_loop(0, heads, second_pass, 0)
+        part[h] = jnp.dot(xt[...], dk, preferred_element_type=F32).reshape(2, 2, seq_block, size)
+        halve(parity, h).start()
+
+    def pairs(body):
+        def both(pair, carry):
+            body(0, 2 * pair)
+            body(1, 2 * pair + 1)
+            return carry
+
+        lax.fori_loop(0, heads // 2, both, 0)
+
+
+    def pass_on(parity, h):
+        halve(parity, h).wait_recv()
+        if parity == 0:
+            passed[h] = part[h, high, other_low] + halved[h, other_low]
+        else:
+            passed[h] = part[h, other_high, low] + halved[h, other_high]
+        quarter(parity, h).start()
+
+    def reduce(parity, h):
+        kept = part[h, high, low] + halved[h, low if parity == 0 else high]
+        quarter(parity, h).wait_recv()
+        reduced[h] = kept + quartered[h]
+
+        def send(i, carry):
+            z_copy(h, i).start()
+            return carry
+
+        lax.fori_loop(1, nz, send, 0)
+
+    second_pass(0, 0)
+    second_pass(1, 1)
+    for h in range(2, heads):
+        second_pass(h % 2, h)
+        pass_on(h % 2, h - 2)
 
     def flat(i):
         return jnp.concatenate([dqkv[i, h] for h in range(heads)], axis=1)
@@ -275,23 +319,11 @@
     swap_gi = remote(gi_acc.at[sib_rows], gi_recv, e_send.at[0], e_recv.at[0], s, sib)
     swap_gi.start()
 
-    own_seq = pl.ds(pl.multiple_of(s * seq_block, seq_block), seq_block)
-
-    def seq_reduce(h, carry):
-        total = part[h, own_seq, :]
-        for i in range(1, ns):
-            seq_copy(h, i).wait_recv()
-            total += seq_recv[h, i - 1]
-        reduced[h] = total
-
-        def send(i, carry):
-            z_copy(h, i).start()
-            return carry
-
-        lax.fori_loop(1, nz, send, 0)
-        return carry
-
-    lax.fori_loop(0, heads, seq_reduce, 0)
+    for h in range(2, heads):
+        pass_on(h % 2, h)
+        reduce(h % 2, h - 2)
+    for h in range(heads - 2, heads):
+        reduce(h % 2, h)
 
     swap_gi.wait()
     gi_ref[...] = (gi_acc[own_rows, :] + gi_recv[...]).astype(BF16)
@@ -309,32 +341,40 @@
     swap_fin.start()
     gw_ref[:, own_cols] = jnp.where(core == 0, fin[:fin_rows, :], fin[fin_rows:, :])
 
-    def drain(h, carry):
+    def drain(parity, h):
         @pl.when(chip < nz - 1)
         def _():
-            link_a(h).wait_send()
+            link_a(h, 0).wait_send()
+            link_a(h, 1).wait_send()
 
         @pl.when(chip > 0)
         def _():
-            link_b(h).wait_send()
-
-        for i in range(1, ns):
-            seq_copy(h, i).wait_send()
+            link_b(h, 0).wait_send()
+            link_b(h, 1).wait_send()
+
+        halve(parity, h).wait_send()
+        quarter(parity, h).wait_send()
 
         def z_wait(i, carry):
             z_copy(h, i).wait_send()
             return carry
 
         lax.fori_loop(1, nz, z_wait, 0)
-        return carry
-
-    lax.fori_loop(0, heads, drain, 0)
+
+    pairs(drain)
     swap_fin.wait()
     gw_ref[:, sib_cols] = jnp.where(core == 0, fin_recv[:fin_rows, :], fin_recv[fin_rows:, :])
 
 
+def hand_on(gi_in, gw_in, gi_ref, gw_ref):
+    gi_ref[...] = gi_in[...]
+    gw_ref[...] = gw_in[...]
+
+
 def on_device(ns, nz, inputs, w_query, w_key, w_value, damping, grad_out):
     x, g = inputs[0], grad_out[0]
+    if ns != 4 or damping.shape[0] % 4:
+        raise ValueError("seq size")
     tok, width = x.shape
     heads, size = damping.shape[0] // 2, damping.shape[1]
     tokens, half = 2 * tok, heads * size
@@ -367,8 +407,10 @@
             state, state, state, state, state, state,
             rows32, rows32,
             vmem((3, heads, tokens, size), BF16),
-            vmem((heads, width, size), F32),
-            vmem((heads, ns - 1, seq_block, size), F32),
+            vmem((heads, 2, 2, seq_block, size), F32),
+            vmem((heads, 2, seq_block, size), F32),
+            vmem((heads, seq_block, size), F32),
+            vmem((heads, seq_block, size), F32),
             vmem((heads, seq_block, size), F32),
             vmem((heads, nz - 1, z_block, size), F32),
             vmem((z_block, half), F32),
@@ -376,8 +418,8 @@
             vmem((tokens, width), F32),
             vmem((tok, width), F32),
             dma((3,)), dma((2,)), dma((2,)),
-            dma((heads,)), dma((heads,)), dma((heads,)), dma((heads,)),
-            dma((heads, ns - 1)), dma((heads, ns - 1)),
+            dma((heads, 2)), dma((heads, 2)), dma((heads, 2)), dma((heads, 2)),
+            dma((heads, 2)), dma((heads, 2)),
             dma((heads, nz - 1)), dma((heads, nz - 1)),
             dma((2,)), dma((2,)),
         ],
@@ -386,6 +428,16 @@
         ),
         name="mesa_backward",
     )(x, w_query, w_key, w_value, damping, g)
+    grad_inputs, grad_weights = pl.pallas_call(
+        hand_on,
+        out_shape=(
+            jax.ShapeDtypeStruct(grad_inputs.shape, BF16),
+            jax.ShapeDtypeStruct(grad_weights.shape, F32),
+        ),
+        in_specs=[spec, spec],
+        out_specs=(spec, spec),
+        name="hand_on",
+    )(grad_inputs, grad_weights)
     return grad_inputs[None], grad_weights
 
 

time: 68.8 us -> 66.2 us (0.962)
  local copies, waits for them, and re-layouts: 3.24 us -> 0 us
  Pallas kernels: 63.8 us -> 64.8 us
    unnamed x2 -> x0, local copies, waits for them, and re-layouts: 3.24 us -> none
    pallas_call x0 -> x1, Pallas kernels: none -> 1.74 us  [on_device(): pl.pallas_call(hand_on, out_shape=(jax.ShapeDtypeStruct(grad_inputs.shape...]
    pallas_call x1, Pallas kernels: 63.8 us -> 63 us  [on_device(): pl.pallas_call(functools.partial(kernel, ns, nz), out_shape=(jax.ShapeDty...]
where the time goes in v2:
time: 66.2 us; the launch traced here: 65.4 us
  Pallas kernels  64.8 us (98%)
    pallas_call x1, Pallas kernels, on_device(): pl.pallas_call(functools.partial(kernel, ns, nz), out_shape=(jax.ShapeDty...  63 us
    pallas_call x1, Pallas kernels, on_device(): pl.pallas_call(hand_on, out_shape=(jax.ShapeDtypeStruct(grad_inputs.shape...  1.74 us

profile of v2, /device:TPU:0, one launch (start us, length us, event | category | flops | bytes accessed | tf_op | source)
XLA Modules:
  0.0 65.4 jit_solution(1529832175958824227)
XLA Ops:
  0.6 63.0 %mesa_backward.1 = (bf16[128,1024]{1,0:T(8,128)(2,1)}, f32[32,1024]{1,0:T(8,128)}) custom-call(bf16[128,1024]{1,0:T(8,128)(2,1)} %bitcast.3, bf16[1024,1024]{1,0:T(8,128)(2,1)} %wq_ref.1, bf16[1024,1024]{1,0:T(8,128)(2,1)} %wk_ref.1, bf16[1024,1024]{1,0:T(8,128)(2,1)} %wv_ref.1, f32[8,128]{1,0:T(8,128)} %damp_ref.1, bf16[128,1024]{1,0:T(8,128)(2,1)} %bitcast.4), custom_call_target="tpu_custom_call" | custom-call | tf_op jit(solution)/shard_map/mesa_backward/pallas_call | solution.py:391
  63.7 1.7 %hand_on.1 = (bf16[128,1024]{1,0:T(8,128)(2,1)}, f32[32,1024]{1,0:T(8,128)}) custom-call(bf16[128,1024]{1,0:T(8,128)(2,1)} %get-tuple-element.6.gi_in, f32[32,1024]{1,0:T(8,128)} %get-tuple-element.7.gw_in), custom_call_target="tpu_custom_call" | custom-call | tf_op jit(solution)/shard_map/hand_on/pallas_call | solution.py:431
